TPU v7x, 32 devices: a whole 2x2x4 slice. The times are simulated.
32 devices in a mesh: lat: 8 (over z, x), lon: 4 (over y, core).
Axes of the slice: x: 2, y: 2, z: 4, core: 2. Of those that a mesh axis runs over, the one named last changes fastest.
Arguments:
- grid_feat: bfloat16 [32768, 474], P(('lat', 'lon')), may hold values from -6 to 6
- grid_send: int32 [32, 4, 256], P(('lat', 'lon')), may hold values from 0 to 1023
- g2m_sender: int32 [131072], P(('lat', 'lon')), may hold values from 0 to 2047, as said below
- g2m_receiver: int32 [131072], P(('lat', 'lon')), may hold values from 0 to 320, as said below
- g2m_geom: float32 [4, 131072], P(None, ('lat', 'lon')), may hold values from -1 to 1
- mesh_geom: float32 [3, 10240], P(None, ('lat', 'lon')), may hold values from -1 to 1
- mesh_adjacent_lists: int32 [32, 8, 112], P(('lat', 'lon')), may hold values from 0 to 319
- mesh_far: int32 [32, 32, 4], P(('lat', 'lon')), may hold values from 0 to 319
- mesh_sender: int32 [131072], P(('lat', 'lon')), may hold values from 0 to 1343, as said below
- mesh_receiver: int32 [131072], P(('lat', 'lon')), may hold values from 0 to 320, as said below
- mesh_edge_geom: float32 [4, 131072], P(None, ('lat', 'lon')), may hold values from -1 to 1
- embed_in: bfloat16 [474, 512], replicated, may hold values from -0.25 to 0.25
- mesh_in: float32 [3, 512], replicated, may hold values from -3.5 to 3.5
- geo_in: float32 [3, 4, 512], replicated, may hold values from -3 to 3
- pair_in: bfloat16 [3, 4, 512, 512], replicated, may hold values from -0.1875 to 0.1875
- square_out: bfloat16 [8, 512, 512], replicated, may hold values from -0.25 to 0.25
Outputs:
- mesh_out: bfloat16 [10240, 512], P(('lat', 'lon'))
Inputs may be any that keep to these rules, and one draw needn't show every extreme that they name: grid_send[s, d, k] is a local grid row of device s, which it sends to the device that has s as its source for side offset o_d. `g2m_sender`: below 1024, a local grid row of the edge's device; else 1024 + d * 256 + k, a row of received_grid whose source exists. `g2m_receiver`: a local mesh row of the edge's device, or 320 for a padding edge; a device's live edges come first, and some device has all 4096 live. mesh_adjacent_lists[t, d, k] is a local mesh row of device t, which it sends to the device that has t as its source for neighbour offset n_d. mesh_far[t, q, k] is a local mesh row of device t, which it sends to device q. `mesh_sender`: below 320, a local mesh row of the edge's device; else a halo row of the edge's device, and a neighbour's row only where that neighbour exists. `mesh_receiver`: a local mesh row of the edge's device, or 320 for a padding edge; a device's live edges come first, and some device has all 4096 live.
All inputs are finite; a program needn't handle non-finite values.
Results may differ from a plain program's by a relative error of at most 0.015.
Values may be sent and summed in bfloat16 or wider, within the bound.
No kernel may reach another device: no remote copies, remote signals or barrier semaphores. Data moves between devices by JAX's collectives and lax.ppermute only.
A program may use at most 128 MiB of HBM per device.

v0:
```python
import jax
import jax.numpy as jnp
from jax import lax
from jax.sharding import PartitionSpec as P

EPSILON = 1e-05
GRID_OFFSETS = ((-1, 0), (1, 0), (0, -1), (0, 1))


def from_behind(block, axis, distance):
    devices = range(lax.axis_size(axis))
    route = [(i - distance, i) for i in devices if i - distance in devices]
    return lax.ppermute(block, axis, route)


def from_behind_2(block, axis, distance):
    devices = range(lax.axis_size(axis))
    route = [((i - distance) % len(devices), i) for i in devices]
    return lax.ppermute(block, axis, route)


def layer_norm(values):
    centre = values - jnp.mean(values, axis=-1, keepdims=True)
    spread = jnp.mean(centre * centre, axis=-1, keepdims=True)
    return centre * lax.rsqrt(spread + EPSILON)


def two_layer(pre_act, out_weight):
    hidden = jax.nn.silu(pre_act).astype(jnp.bfloat16)
    return layer_norm(jnp.dot(hidden, out_weight, preferred_element_type=jnp.float32))


def edge_sums(sender_term, receiver_term, senders, receivers, geometry, geo_weight, out_weight):
    node_count = receiver_term.shape[0]
    row_ids = jnp.minimum(receivers, node_count - 1)
    pre_act = jnp.dot(geometry.T, geo_weight, precision=lax.Precision.HIGHEST)
    pre_act = pre_act + sender_term[senders] + receiver_term[row_ids]
    message = two_layer(pre_act, out_weight).astype(jnp.bfloat16)
    incidence = (receivers[None, :] == jnp.arange(node_count, dtype=jnp.int32)[:, None]).astype(
        jnp.bfloat16
    )
    return jnp.dot(incidence, message, preferred_element_type=jnp.float32)


def node_update(latent, edge_sum, section_weights, out_weight):
    pre_act = jnp.dot(latent, section_weights[2], preferred_element_type=jnp.float32)
    pre_act = pre_act + jnp.dot(
        edge_sum.astype(jnp.bfloat16), section_weights[3], preferred_element_type=jnp.float32
    )
    return (latent.astype(jnp.float32) + two_layer(pre_act, out_weight)).astype(jnp.bfloat16)


def per_device(
    grid_feat,
    grid_send,
    g2m_sender,
    g2m_receiver,
    g2m_geom,
    mesh_geom,
    mesh_adjacent_lists,
    mesh_far,
    mesh_sender,
    mesh_receiver,
    mesh_edge_geom,
    embed_in,
    mesh_in,
    geo_in,
    pair_in,
    square_out,
):
    feature_width = embed_in.shape[1]
    outgoing_ids = grid_send[0]
    pre_act = jnp.dot(grid_feat, embed_in, preferred_element_type=jnp.float32)
    grid_latent = two_layer(pre_act, square_out[0]).astype(jnp.bfloat16)
    outgoing = grid_latent[outgoing_ids]
    arrived = []
    for offset_id, (lat_step, lon_step) in enumerate(GRID_OFFSETS):
        if lat_step != 0:
            moved = from_behind(outgoing[offset_id], "lat", lat_step)
        else:
            moved = from_behind_2(outgoing[offset_id], "lon", lon_step)
        arrived.append(moved)
    received_grid = jnp.concatenate([grid_latent] + arrived, axis=0)
    sender_term = jnp.dot(received_grid, pair_in[0, 0], preferred_element_type=jnp.float32)
    mesh_first = jnp.dot(mesh_geom.T, mesh_in, precision=lax.Precision.HIGHEST)
    mesh_start = two_layer(mesh_first, square_out[1]).astype(jnp.bfloat16)
    receiver_term = jnp.dot(mesh_start, pair_in[0, 1], preferred_element_type=jnp.float32)
    edge_sum = edge_sums(
        sender_term, receiver_term, g2m_sender, g2m_receiver, g2m_geom, geo_in[0], square_out[2]
    )
    mesh_latent = node_update(mesh_start, edge_sum, pair_in[0], square_out[3])
    near_ids = mesh_adjacent_lists[0]
    far_ids = mesh_far[0]
    for section_id in range(1, geo_in.shape[0]):
        near_out = mesh_latent[near_ids]
        banded = {}
        for lat_step in (-1, 1):
            first = 0 if lat_step < 0 else 5
            banded[lat_step] = from_behind(near_out[first : first + 3], "lat", lat_step)
        columns = {}
        for lon_step in (-1, 1):
            side = 0 if lon_step < 0 else 2
            own_slot = 3 if lon_step < 0 else 4
            stacked = jnp.stack([near_out[own_slot], banded[-1][side], banded[1][side]], axis=0)
            columns[lon_step] = from_behind_2(stacked, "lon", lon_step)
        near_blocks = [
            columns[-1][1],
            banded[-1][1],
            columns[1][1],
            columns[-1][0],
            columns[1][0],
            columns[-1][2],
            banded[1][1],
            columns[1][2],
        ]
        far_out = mesh_latent[far_ids]
        far_in = lax.all_to_all(far_out, ("lat", "lon"), split_axis=0, concat_axis=0, tiled=True)
        sender_table = jnp.concatenate(
            [mesh_latent] + near_blocks + [far_in.reshape(-1, feature_width)], axis=0
        )
        sender_term = jnp.dot(
            sender_table, pair_in[section_id, 0], preferred_element_type=jnp.float32
        )
        receiver_term = jnp.dot(
            mesh_latent, pair_in[section_id, 1], preferred_element_type=jnp.float32
        )
        edge_sum = edge_sums(
            sender_term,
            receiver_term,
            mesh_sender,
            mesh_receiver,
            mesh_edge_geom,
            geo_in[section_id],
            square_out[2 + 2 * section_id],
        )
        mesh_latent = node_update(
            mesh_latent, edge_sum, pair_in[section_id], square_out[3 + 2 * section_id]
        )
    return mesh_latent


def solution(mesh):
    in_specs = (
        P(("lat", "lon"), None),
        P(("lat", "lon"), None, None),
        P(("lat", "lon")),
        P(("lat", "lon")),
        P(None, ("lat", "lon")),
        P(None, ("lat", "lon")),
        P(("lat", "lon"), None, None),
        P(("lat", "lon"), None, None),
        P(("lat", "lon")),
        P(("lat", "lon")),
        P(None, ("lat", "lon")),
        P(),
        P(),
        P(),
        P(),
        P(),
    )
    out_specs = P(("lat", "lon"), None)
    return jax.shard_map(
        per_device, mesh=mesh, in_specs=in_specs, out_specs=out_specs, check_vma=False
    )
```

profile of v0, /device:TPU:0, one launch (start us, length us, event | category | flops | bytes accessed | tf_op | source)
XLA Modules:
  0.0 304.4 jit_solution(4767106620007408679)
XLA Ops:
  7.6 4.0 %gather_fusion = bf16[1024,512]{1,0:T(8,128)(2,1)S(1)} fusion(bf16[1024,512]{1,0:T(8,128)(2,1)S(1)} %copy.23, s32[1024]{0:T(1024)S(1)} %broadcast_clamp_fusion), kind=kCustom, calls=%fused_computation | custom fusion | bytes 2101248 | tf_op jit(solution)/shard_map/gather | solution.py:75
  14.7 6.2 %collective-permute-start.1 = (bf16[256,512]{0,1:T(8,128)(2,1)}, bf16[256,512]{0,1:T(8,128)(2,1)}, u32[]{:S(2)}, u32[]{:S(2)}) collective-permute-start(bf16[256,512]{0,1:T(8,128)(2,1)} %copy.30), channel_id=1, source_target_pairs={{0,4},{4,8},{8,12},{12,16},{16,20},{20,24},{24,28},{1,5},{5,9},{9,... | collective-permute-start | bytes 786440 | tf_op jit(solution)/shard_map/ppermute | solution.py:13
  30.0 9.1 %fusion.94 = f32[4096,512]{1,0:T(8,128)} fusion(f32[4,4096]{1,0:T(4,128)S(1)} %copy-done.9, f32[3,4,512]{2,1,0:T(4,128)S(1)} %copy-done.16), kind=kOutput, calls=%fused_computation.176 | convolution fusion | flops 100663296 | bytes 8462336 | tf_op jit(solution)/shard_map/dot_general | solution.py:36
  39.5 16.8 %gather_fusion.2 = f32[4096,512]{1,0:T(8,128)} fusion(f32[320,512]{1,0:T(8,128)S(1)} %fusion.43, s32[4096]{0:T(1024)S(1)} %get-tuple-element.48), kind=kCustom, calls=%fused_computation.2 | custom fusion | bytes 16793600 | tf_op jit(solution)/shard_map/gather | solution.py:37
  60.2 4.3 %fusion.45 = f32[2048,512]{1,0:T(8,128)} fusion(bf16[2048,512]{0,1:T(8,128)(2,1)S(1)} %constant_dynamic-update-slice_fusion, bf16[3,4,512,512]{3,2,1,0:T(8,128)(2,1)} %param.30), kind=kOutput, calls=%fused_computation.85 | convolution fusion | flops 1073741824 | bytes 6815744 | tf_op jit(solution)/shard_map/dot_general | solution.py:84
  64.5 20.2 %gather_fusion.1 = f32[4096,512]{1,0:T(8,128)} fusion(f32[2048,512]{1,0:T(8,128)} %fusion.45, s32[4096]{0:T(1024)S(1)} %get-tuple-element.47), kind=kCustom, calls=%fused_computation.1 | custom fusion | bytes 16793600 | tf_op jit(solution)/shard_map/gather | solution.py:37
  84.7 10.1 %fusion.111 = (f32[4096]{0:T(1024)S(1)}, f32[4096,512]{0,1:T(8,128)S(1)}) fusion(bf16[8,512,512]{2,1,0:T(8,128)(2,1)} %param.31, f32[4096,512]{1,0:T(8,128)} %gather_fusion.2, f32[4096,512]{1,0:T(8,128)} %fusion.94, f32[4096,512]{1,0:T(8,128)} %gather_fusion.1), kind=kOutput, calls=%fused_computation.210 | convolution fusion | flops 2164256768 | bytes 34095104 | tf_op jit(solution)/shard_map/dot_general | solution.py:30
  98.0 5.4 %multiply_convert_fusion.31 = bf16[320,512]{1,0:T(8,128)(2,1)S(1)} fusion(f32[320,512]{1,0:T(8,128)S(1)} %copy-done.6, f32[4096,512]{0,1:T(8,128)} %copy-done.4, f32[4096]{0:T(1024)S(1)} %add_rsqrt_fusion.2, f32[4096]{0:T(1024)S(1)} %broadcast_multiply_fusion.2, s32[4096]{0:T(1024)S(1)} %copy-done.12, bf16[3,4,512,512]{3,2,1,0:T(8,128)(2,1)} %param.30), kind=kOutput, calls=%fused_computation.53 | convolution fusion | flops 1518698496 | bytes 9945088 | tf_op jit(solution)/shard_map/dot_general | solution.py:47
  113.2 5.0 %collective-permute-start.5 = (bf16[3,112,512]{2,1,0:T(8,128)(2,1)S(1)}, bf16[3,112,512]{2,1,0:T(8,128)(2,1)S(1)}, u32[]{:S(2)}, u32[]{:S(2)}) collective-permute-start(bf16[3,112,512]{2,1,0:T(8,128)(2,1)S(1)} %bitcast.198), channel_id=1, source_target_pairs={{0,4},{4,8},{8,12},{12,16},{16,20},{20,24},{24,28},{1,5},{5,9},{9,... | collective-permute-start | bytes 1032200 | tf_op jit(solution)/shard_map/ppermute | solution.py:13
  119.7 6.0 %all-to-all-start = ((bf16[32,4,512]{2,1,0:T(4,128)(2,1)}), bf16[32,4,512]{2,1,0:T(4,128)(2,1)S(1)}, u32[]{:S(2)}, u32[]{:S(2)}) async-start(bf16[32,4,512]{2,1,0:T(4,128)(2,1)} %reshape.235), calls=%async_computation | async-start | bytes 262144 | tf_op jit(solution)/shard_map/all_to_all | solution.py:117
  125.8 16.8 %gather_fusion.6 = f32[4096,512]{1,0:T(8,128)} fusion(f32[320,512]{1,0:T(8,128)S(1)} %fusion.33, s32[4096]{0:T(1024)S(1)} %get-tuple-element.50), kind=kCustom, calls=%fused_computation.6 | custom fusion | bytes 16793600 | tf_op jit(solution)/shard_map/gather | solution.py:37
  146.6 3.8 %collective-permute-done.6 = bf16[3,112,512]{2,1,0:T(8,128)(2,1)S(1)} collective-permute-done((bf16[3,112,512]{2,1,0:T(8,128)(2,1)S(1)}, bf16[3,112,512]{2,1,0:T(8,128)(2,1)S(1)}, u32[]{:S(2)}, u32[]{:S(2)}) %collective-permute-start.6) | collective-permute-done | bytes 344096 | tf_op jit(solution)/shard_map/ppermute | solution.py:19
  160.4 16.8 %gather_fusion.5 = f32[4096,512]{1,0:T(8,128)} fusion(f32[1344,512]{1,0:T(8,128)S(1)} %fusion.35, s32[4096]{0:T(1024)S(1)} %get-tuple-element.49), kind=kCustom, calls=%fused_computation.5 | custom fusion | bytes 16793600 | tf_op jit(solution)/shard_map/gather | solution.py:37
  177.2 12.3 %multiply_convert_fusion.3 = bf16[4096,512]{1,0:T(8,128)(2,1)S(1)} fusion(f32[4096,512]{1,0:T(8,128)} %gather_fusion.6, f32[4096,512]{1,0:T(8,128)} %gather_fusion.5, f32[4,4096]{1,0:T(4,128)S(1)} %copy-done.18, f32[3,4,512]{2,1,0:T(4,128)S(1)} %copy-done.16), kind=kOutput, calls=%fused_computation.16 | convolution fusion | flops 115343360 | bytes 21045248 | tf_op jit(solution)/shard_map/dot_general | solution.py:36
  189.5 3.5 %fusion.113 = (f32[4096]{0:T(1024)S(1)}, f32[4096,512]{0,1:T(8,128)S(1)}) fusion(bf16[4096,512]{1,0:T(8,128)(2,1)S(1)} %multiply_convert_fusion.3, bf16[8,512,512]{2,1,0:T(8,128)(2,1)} %param.31), kind=kOutput, calls=%fused_computation.212 | convolution fusion | flops 2149576704 | bytes 13123584 | tf_op jit(solution)/shard_map/dot_general | solution.py:30
  197.4 5.4 %multiply_convert_fusion.28 = bf16[320,512]{1,0:T(8,128)(2,1)S(1)} fusion(f32[320,512]{1,0:T(8,128)S(1)} %copy-done.7, f32[4096,512]{0,1:T(8,128)} %copy-done.2, f32[4096]{0:T(1024)S(1)} %add_rsqrt_fusion.1, f32[4096]{0:T(1024)S(1)} %broadcast_multiply_fusion.1, s32[4096]{0:T(1024)S(1)} %copy-done.13, bf16[3,4,512,512]{3,2,1,0:T(8,128)(2,1)} %param.30), kind=kOutput, calls=%fused_computation.50 | convolution fusion | flops 1518698496 | bytes 9945088 | tf_op jit(solution)/shard_map/dot_general | solution.py:47
  212.5 4.7 %collective-permute-start.9 = (bf16[3,112,512]{2,1,0:T(8,128)(2,1)S(1)}, bf16[3,112,512]{2,1,0:T(8,128)(2,1)S(1)}, u32[]{:S(2)}, u32[]{:S(2)}) collective-permute-start(bf16[3,112,512]{2,1,0:T(8,128)(2,1)S(1)} %bitcast.197), channel_id=1, source_target_pairs={{0,4},{4,8},{8,12},{12,16},{16,20},{20,24},{24,28},{1,5},{5,9},{9,... | collective-permute-start | bytes 1032200 | tf_op jit(solution)/shard_map/ppermute | solution.py:13
  218.8 5.6 %all-to-all-start.1 = ((bf16[32,4,512]{2,1,0:T(4,128)(2,1)}), bf16[32,4,512]{2,1,0:T(4,128)(2,1)S(1)}, u32[]{:S(2)}, u32[]{:S(2)}) async-start(bf16[32,4,512]{2,1,0:T(4,128)(2,1)} %reshape.267), calls=%async_computation.1 | async-start | bytes 262144 | tf_op jit(solution)/shard_map/all_to_all | solution.py:117
  224.4 16.8 %gather_fusion.10 = f32[4096,512]{1,0:T(8,128)} fusion(f32[320,512]{1,0:T(8,128)S(1)} %fusion.22, s32[4096]{0:T(1024)S(1)} %get-tuple-element.50), kind=kCustom, calls=%fused_computation.10 | custom fusion | bytes 16793600 | tf_op jit(solution)/shard_map/gather | solution.py:37
  245.3 3.8 %collective-permute-done.10 = bf16[3,112,512]{2,1,0:T(8,128)(2,1)S(1)} collective-permute-done((bf16[3,112,512]{2,1,0:T(8,128)(2,1)S(1)}, bf16[3,112,512]{2,1,0:T(8,128)(2,1)S(1)}, u32[]{:S(2)}, u32[]{:S(2)}) %collective-permute-start.10) | collective-permute-done | bytes 344096 | tf_op jit(solution)/shard_map/ppermute | solution.py:19
  259.1 16.8 %gather_fusion.9 = f32[4096,512]{1,0:T(8,128)} fusion(f32[1344,512]{1,0:T(8,128)S(1)} %fusion.24, s32[4096]{0:T(1024)S(1)} %get-tuple-element.49), kind=kCustom, calls=%fused_computation.9 | custom fusion | bytes 16793600 | tf_op jit(solution)/shard_map/gather | solution.py:37
  275.9 12.3 %multiply_convert_fusion.1 = bf16[4096,512]{1,0:T(8,128)(2,1)S(1)} fusion(f32[4096,512]{1,0:T(8,128)} %gather_fusion.10, f32[4096,512]{1,0:T(8,128)} %gather_fusion.9, f32[4,4096]{1,0:T(4,128)S(1)} %copy-done.19, f32[3,4,512]{2,1,0:T(4,128)S(1)} %copy-done.16), kind=kOutput, calls=%fused_computation.13 | convolution fusion | flops 115343360 | bytes 21045248 | tf_op jit(solution)/shard_map/dot_general | solution.py:36
  288.2 3.5 %fusion.115 = (f32[4096]{0:T(1024)S(1)}, f32[4096,512]{0,1:T(8,128)S(1)}) fusion(bf16[4096,512]{1,0:T(8,128)(2,1)S(1)} %multiply_convert_fusion.1, bf16[8,512,512]{2,1,0:T(8,128)(2,1)} %param.31), kind=kOutput, calls=%fused_computation.214 | convolution fusion | flops 2149576704 | bytes 13123584 | tf_op jit(solution)/shard_map/dot_general | solution.py:30
  296.1 5.5 %multiply_convert_fusion.25 = bf16[320,512]{1,0:T(8,128)(2,1)S(1)} fusion(f32[320,512]{1,0:T(8,128)S(1)} %copy-done.8, f32[4096,512]{0,1:T(8,128)} %copy-done.3, f32[4096]{0:T(1024)S(1)} %add_rsqrt_fusion, f32[4096]{0:T(1024)S(1)} %broadcast_multiply_fusion, s32[4096]{0:T(1024)S(1)} %copy-done.13, bf16[3,4,512,512]{3,2,1,0:T(8,128)(2,1)} %param.30), kind=kOutput, calls=%fused_computation.47 | convolution fusion | flops 1518698496 | bytes 9945088 | tf_op jit(solution)/shard_map/dot_general | solution.py:47
  (166 shorter events, 88.7 us)
Async XLA Ops:
  11.6 12.0 %copy-start.20 = (f32[3,512]{1,0:T(4,128)S(1)}, f32[3,512]{1,0:T(4,128)}, u32[]{:S(2)}) copy-start(f32[3,512]{1,0:T(4,128)} %param.28) | copy-start | bytes 18436
  11.6 12.0 %copy-start.21 = (f32[3,320]{1,0:T(4,128)S(1)}, f32[3,320]{1,0:T(4,128)}, u32[]{:S(2)}) copy-start(f32[3,320]{1,0:T(4,128)} %param.21) | copy-start | bytes 11524
  12.6 43.7 %collective-permute-start = (bf16[256,512]{0,1:T(8,128)(2,1)}, bf16[256,512]{0,1:T(8,128)(2,1)}, u32[]{:S(2)}, u32[]{:S(2)}) collective-permute-start(bf16[256,512]{0,1:T(8,128)(2,1)} %copy.29), channel_id=1, source_target_pairs={{4,0},{8,4},{12,8},{16,12},{20,16},{24,20},{28,24},{5,1},{9,5},{13... | collective-permute-start | bytes 786440 | tf_op jit(solution)/shard_map/ppermute | solution.py:13
  14.7 42.5 %collective-permute-start.1 = (bf16[256,512]{0,1:T(8,128)(2,1)}, bf16[256,512]{0,1:T(8,128)(2,1)}, u32[]{:S(2)}, u32[]{:S(2)}) collective-permute-start(bf16[256,512]{0,1:T(8,128)(2,1)} %copy.30), channel_id=1, source_target_pairs={{0,4},{4,8},{8,12},{12,16},{16,20},{20,24},{24,28},{1,5},{5,9},{9,... | collective-permute-start | bytes 786440 | tf_op jit(solution)/shard_map/ppermute | solution.py:13
  21.7 36.5 %collective-permute-start.2 = (bf16[256,512]{0,1:T(8,128)(2,1)}, bf16[256,512]{0,1:T(8,128)(2,1)}, u32[]{:S(2)}, u32[]{:S(2)}) collective-permute-start(bf16[256,512]{0,1:T(8,128)(2,1)} %copy.31), channel_id=1, source_target_pairs={{1,0},{2,1},{3,2},{0,3},{5,4},{6,5},{7,6},{4,7},{9,8},{10,9},{11,1... | collective-permute-start | bytes 786440 | tf_op jit(solution)/shard_map/ppermute | solution.py:19
  23.5 6.5 %copy-start.16 = (f32[3,4,512]{2,1,0:T(4,128)S(1)}, f32[3,4,512]{2,1,0:T(4,128)}, u32[]{:S(2)}) copy-start(f32[3,4,512]{2,1,0:T(4,128)} %param.29) | copy-start | bytes 73732
  23.5 35.7 %collective-permute-start.3 = (bf16[256,512]{0,1:T(8,128)(2,1)}, bf16[256,512]{0,1:T(8,128)(2,1)}, u32[]{:S(2)}, u32[]{:S(2)}) collective-permute-start(bf16[256,512]{0,1:T(8,128)(2,1)} %copy.32), channel_id=1, source_target_pairs={{3,0},{0,1},{1,2},{2,3},{7,4},{4,5},{5,6},{6,7},{11,8},{8,9},{9,10... | collective-permute-start | bytes 786440 | tf_op jit(solution)/shard_map/ppermute | solution.py:19
  30.0 9.1 %copy-start.11 = (s32[4096]{0:T(1024)S(1)}, s32[4096]{0:T(1024)}, u32[]{:S(2)}) copy-start(s32[4096]{0:T(1024)} %param.24) | copy-start | bytes 49156
  30.0 9.1 %copy-start.13 = (s32[4096]{0:T(1024)S(1)}, s32[4096]{0:T(1024)}, u32[]{:S(2)}) copy-start(s32[4096]{0:T(1024)} %param.25) | copy-start | bytes 49156
  30.0 9.1 %copy-start.17 = (s32[1,32,4]{1,2,0:T(4,128)S(1)}, s32[1,32,4]{1,2,0:T(4,128)}, u32[]{:S(2)}) copy-start(s32[1,32,4]{1,2,0:T(4,128)} %param.23) | copy-start | bytes 1540
  39.5 16.8 %copy-start.5 = (bf16[2048,512]{0,1:T(8,128)(2,1)S(1)}, bf16[2048,512]{0,1:T(8,128)(2,1)}, u32[]{:S(2)}) copy-start(bf16[2048,512]{0,1:T(8,128)(2,1)} %get-tuple-element.9) | copy-start | bytes 6291460
  110.5 32.0 %collective-permute-start.4 = (bf16[3,112,512]{2,1,0:T(8,128)(2,1)}, bf16[3,112,512]{2,1,0:T(8,128)(2,1)S(1)}, u32[]{:S(2)}, u32[]{:S(2)}) collective-permute-start(bf16[3,112,512]{2,1,0:T(8,128)(2,1)} %bitcast.14), channel_id=1, source_target_pairs={{4,0},{8,4},{12,8},{16,12},{20,16},{24,20},{28,24},{5,1},{9,5},{13... | collective-permute-start | bytes 1032200 | tf_op jit(solution)/shard_map/ppermute | solution.py:13
  113.2 29.3 %collective-permute-start.5 = (bf16[3,112,512]{2,1,0:T(8,128)(2,1)S(1)}, bf16[3,112,512]{2,1,0:T(8,128)(2,1)S(1)}, u32[]{:S(2)}, u32[]{:S(2)}) collective-permute-start(bf16[3,112,512]{2,1,0:T(8,128)(2,1)S(1)} %bitcast.198), channel_id=1, source_target_pairs={{0,4},{4,8},{8,12},{12,16},{16,20},{20,24},{24,28},{1,5},{5,9},{9,... | collective-permute-start | bytes 1032200 | tf_op jit(solution)/shard_map/ppermute | solution.py:13
  119.7 26.7 %all-to-all-start = ((bf16[32,4,512]{2,1,0:T(4,128)(2,1)}), bf16[32,4,512]{2,1,0:T(4,128)(2,1)S(1)}, u32[]{:S(2)}, u32[]{:S(2)}) async-start(bf16[32,4,512]{2,1,0:T(4,128)(2,1)} %reshape.235), calls=%async_computation | async-start | bytes 262144 | tf_op jit(solution)/shard_map/all_to_all | solution.py:117
  142.6 7.8 %collective-permute-start.6 = (bf16[3,112,512]{2,1,0:T(8,128)(2,1)S(1)}, bf16[3,112,512]{2,1,0:T(8,128)(2,1)S(1)}, u32[]{:S(2)}, u32[]{:S(2)}) collective-permute-start(bf16[3,112,512]{2,1,0:T(8,128)(2,1)S(1)} %pad_maximum_fusion), channel_id=1, source_target_pairs={{1,0},{2,1},{3,2},{0,3},{5,4},{6,5},{7,6},{4,7},{9,8},{10,9},{11,1... | collective-permute-start | bytes 1032200 | tf_op jit(solution)/shard_map/ppermute | solution.py:19
  146.5 6.9 %collective-permute-start.7 = (bf16[3,112,512]{2,1,0:T(8,128)(2,1)S(1)}, bf16[3,112,512]{2,1,0:T(8,128)(2,1)S(1)}, u32[]{:S(2)}, u32[]{:S(2)}) collective-permute-start(bf16[3,112,512]{2,1,0:T(8,128)(2,1)S(1)} %pad_maximum_fusion.1), channel_id=1, source_target_pairs={{3,0},{0,1},{1,2},{2,3},{7,4},{4,5},{5,6},{6,7},{11,8},{8,9},{9,10... | collective-permute-start | bytes 1032200 | tf_op jit(solution)/shard_map/ppermute | solution.py:19
  160.4 16.8 %copy-start.18 = (f32[4,4096]{1,0:T(4,128)S(1)}, f32[4,4096]{1,0:T(4,128)}, u32[]{:S(2)}) copy-start(f32[4,4096]{1,0:T(4,128)} %param.26) | copy-start | bytes 196612
  209.8 31.4 %collective-permute-start.8 = (bf16[3,112,512]{2,1,0:T(8,128)(2,1)}, bf16[3,112,512]{2,1,0:T(8,128)(2,1)S(1)}, u32[]{:S(2)}, u32[]{:S(2)}) collective-permute-start(bf16[3,112,512]{2,1,0:T(8,128)(2,1)} %bitcast.34), channel_id=1, source_target_pairs={{4,0},{8,4},{12,8},{16,12},{20,16},{24,20},{28,24},{5,1},{9,5},{13... | collective-permute-start | bytes 1032200 | tf_op jit(solution)/shard_map/ppermute | solution.py:13
  212.5 28.8 %collective-permute-start.9 = (bf16[3,112,512]{2,1,0:T(8,128)(2,1)S(1)}, bf16[3,112,512]{2,1,0:T(8,128)(2,1)S(1)}, u32[]{:S(2)}, u32[]{:S(2)}) collective-permute-start(bf16[3,112,512]{2,1,0:T(8,128)(2,1)S(1)} %bitcast.197), channel_id=1, source_target_pairs={{0,4},{4,8},{8,12},{12,16},{16,20},{20,24},{24,28},{1,5},{5,9},{9,... | collective-permute-start | bytes 1032200 | tf_op jit(solution)/shard_map/ppermute | solution.py:13
  218.8 26.3 %all-to-all-start.1 = ((bf16[32,4,512]{2,1,0:T(4,128)(2,1)}), bf16[32,4,512]{2,1,0:T(4,128)(2,1)S(1)}, u32[]{:S(2)}, u32[]{:S(2)}) async-start(bf16[32,4,512]{2,1,0:T(4,128)(2,1)} %reshape.267), calls=%async_computation.1 | async-start | bytes 262144 | tf_op jit(solution)/shard_map/all_to_all | solution.py:117
  241.3 7.8 %collective-permute-start.10 = (bf16[3,112,512]{2,1,0:T(8,128)(2,1)S(1)}, bf16[3,112,512]{2,1,0:T(8,128)(2,1)S(1)}, u32[]{:S(2)}, u32[]{:S(2)}) collective-permute-start(bf16[3,112,512]{2,1,0:T(8,128)(2,1)S(1)} %pad_maximum_fusion.2), channel_id=1, source_target_pairs={{1,0},{2,1},{3,2},{0,3},{5,4},{6,5},{7,6},{4,7},{9,8},{10,9},{11,1... | collective-permute-start | bytes 1032200 | tf_op jit(solution)/shard_map/ppermute | solution.py:19
  245.2 6.9 %collective-permute-start.11 = (bf16[3,112,512]{2,1,0:T(8,128)(2,1)S(1)}, bf16[3,112,512]{2,1,0:T(8,128)(2,1)S(1)}, u32[]{:S(2)}, u32[]{:S(2)}) collective-permute-start(bf16[3,112,512]{2,1,0:T(8,128)(2,1)S(1)} %pad_maximum_fusion.3), channel_id=1, source_target_pairs={{3,0},{0,1},{1,2},{2,3},{7,4},{4,5},{5,6},{6,7},{11,8},{8,9},{9,10... | collective-permute-start | bytes 1032200 | tf_op jit(solution)/shard_map/ppermute | solution.py:19
  259.1 16.8 %copy-start.19 = (f32[4,4096]{1,0:T(4,128)S(1)}, f32[4,4096]{1,0:T(4,128)}, u32[]{:S(2)}) copy-start(f32[4,4096]{1,0:T(4,128)} %param.26) | copy-start | bytes 196612
  296.1 8.2 %copy-start.1 = (bf16[1024,474]{0,1:T(8,128)(2,1)S(1)}, bf16[1024,474]{0,1:T(8,128)(2,1)}, u32[]{:S(2)}) copy-start(bf16[1024,474]{0,1:T(8,128)(2,1)} %param.16) | copy-start | bytes 2912260
  (12 other events, 45.7 us)
where the time goes:
time: 310 us; the launch traced here: 304 us
  local copies, waits for them, and re-layouts  151 us (49%)
  matrix products  96.8 us (31%)
  starting transfers between devices  35.6 us (11%)
  waiting for transfers between devices  11.2 us (4%)
  other arithmetic  9.27 us (3%)
    gather x6, local copies, waits for them, and re-layouts, edge_sums(): pre_act = pre_act + sender_term[senders] + receiver_term[row_ids]  104 us
    dot_general x3, matrix products, edge_sums(): pre_act = jnp.dot(geometry.T, geo_weight, precision=lax.Precision.HIGHEST)  33.7 us
    unnamed x68, local copies, waits for them, and re-layouts  26.8 us
    dot_general x8, matrix products, two_layer(): jnp.dot(hidden, out_weight, preferred_element_type=jnp.float32)  25.9 us
    ppermute x6, starting transfers between devices, from_behind(): return lax.ppermute(block, axis, route)  19.7 us
    dot_general x3, matrix products, node_update(): jnp.dot(edge_sum.astype(jnp.bfloat16), section_weights[3], preferred_elem...  16.4 us
    all_to_all x2, starting transfers between devices, per_device(): lax.all_to_all(far_out, ('lat', 'lon'), split_axis=0, concat_axis=0, tile...  11.6 us
    ppermute x6, waiting for transfers between devices, from_behind_2(): return lax.ppermute(block, axis, route)  11.1 us
  transfers between devices with their start and end apart: 14, of which 4 were waited for; matrix products, arithmetic and copies ran while one was open for 28% of the time, Pallas kernels for 0%

commit v1 on v0

v1 whole, which is shorter than its diff:
```python
import functools

import jax
import jax.numpy as jnp
from jax import lax
from jax.experimental import pallas as pl
from jax.experimental.pallas import tpu as pltpu
from jax.sharding import PartitionSpec as P

EPSILON = 1e-05
TILE = 256
WINDOW = 256
LANES = 128
GEO_ROWS = 16
AXES = ("lat", "lon")
BF16 = jnp.bfloat16
F32 = jnp.float32
NT = (((1,), (1,)), ((), ()))


def up(n, m):
    return -(-n // m) * m


def mm(a, b):
    return jnp.dot(a, b, preferred_element_type=F32)


def mm_nt(a, b):
    return lax.dot_general(a, b, NT, preferred_element_type=F32)


def silu_bf16(x):
    half = 0.5 * x
    return (half + half * jnp.tanh(half)).astype(BF16)


def norm(values, axis):
    scale = 1.0 / values.shape[axis]
    centre = values - jnp.sum(values, axis=axis, keepdims=True) * scale
    spread = jnp.sum(centre * centre, axis=axis, keepdims=True) * scale
    return centre * lax.rsqrt(spread + EPSILON)


def one_hot_rows(ids, count):
    rows = lax.broadcasted_iota(jnp.int32, (count, ids.shape[1]), 0)
    return (rows == ids).astype(F32).astype(BF16)


def edge_tiles(first, last, lo_ref, hi_ref, key_ref, geo_ref, st_ref, rg_ref, wo_ref, acc_ref, pre_ref, shift):
    node_count = acc_ref.shape[0]

    def one_tile(tile, carry):
        lanes = pl.ds(pl.multiple_of(tile * TILE, TILE), TILE)
        key = key_ref[:, lanes]
        sender = lax.shift_right_logical(key, shift)
        receiver = key & ((1 << shift) - 1)
        incidence = one_hot_rows(receiver, node_count)
        base = (lo_ref[tile] // LANES) * LANES
        windows = (hi_ref[tile] - base) // WINDOW + 1

        def window(start):
            start = pl.multiple_of(start, LANES)
            return mm(st_ref[:, pl.ds(start, WINDOW)], one_hot_rows(sender - start, WINDOW))

        pre_ref[...] = mm(
            rg_ref[...], jnp.concatenate([incidence, geo_ref[:, lanes]], axis=0)
        ) + window(base)

        @pl.when(windows > 1)
        def _():
            def more(i, c):
                pre_ref[...] += window(base + i * WINDOW)
                return c

            lax.fori_loop(1, windows, more, 0)

        message = norm(mm(wo_ref[...], silu_bf16(pre_ref[...])), 0).astype(BF16)
        acc_ref[...] += mm_nt(incidence, message)
        return carry

    lax.fori_loop(first, last, one_tile, 0)


def pick_kernel(ids_ref, table_ref, out_ref):
    rows = table_ref.shape[0]
    for part in range(ids_ref.shape[0]):
        wide = jnp.broadcast_to(ids_ref[part : part + 1, :].astype(F32), (LANES, LANES))
        column = wide.T[:, :1].astype(jnp.int32)
        hot = (lax.broadcasted_iota(jnp.int32, (LANES, rows), 1) == column).astype(F32).astype(BF16)
        out_ref[part * LANES : (part + 1) * LANES, :] = mm(hot, table_ref[...]).astype(BF16)


def embed_grid(rows_ref, embed_ref, square_ref, wst_ref, st_ref, lane_offset):
    chunk = 256
    for part in range(rows_ref.shape[0] // chunk):
        hidden = silu_bf16(mm(rows_ref[part * chunk : (part + 1) * chunk, :], embed_ref[...]))
        latent = norm(mm(hidden, square_ref[0]), 1).astype(BF16)
        at = lane_offset + part * chunk
        st_ref[:, at : at + chunk] = mm_nt(wst_ref[...], latent).astype(BF16)


def fill_receivers(rg_ref, latent, weight_t, wg_ref):
    nodes = latent.shape[0]
    rg_ref[:, :nodes] = mm_nt(weight_t, latent).astype(BF16)
    rg_ref[:, nodes:] = wg_ref[0]


def first_encoder_kernel(shift, cut_ref, lo_ref, hi_ref, key_ref, geo_ref, grid_ref, mesh_geom_ref, embed_ref, mesh_in_ref,
                         square_grid_ref, square_mesh_ref, square_edge_ref, pair_ref, wg_ref,
                         st_ref, rg_ref, acc_ref, wst_ref, wo_ref, start_ref, pre_ref):
    wst_ref[...] = pair_ref[0, 0].T
    wo_ref[...] = square_edge_ref[0].T
    own = grid_ref.shape[0]
    st_ref[:, own:] = jnp.zeros((st_ref.shape[0], st_ref.shape[1] - own), BF16)
    embed_grid(grid_ref, embed_ref, square_grid_ref, wst_ref, st_ref, 0)
    geom = mesh_geom_ref[...]
    first = geom[:, 0:1] * mesh_in_ref[0:1, :]
    for k in range(1, geom.shape[1]):
        first = first + geom[:, k : k + 1] * mesh_in_ref[k : k + 1, :]
    start = norm(mm(silu_bf16(first), square_mesh_ref[0]), 1).astype(BF16)
    start_ref[...] = start
    fill_receivers(rg_ref, start, pair_ref[0, 1].T, wg_ref)
    acc_ref[...] = jnp.zeros_like(acc_ref)
    edge_tiles(0, cut_ref[0], lo_ref, hi_ref, key_ref, geo_ref, st_ref, rg_ref, wo_ref, acc_ref, pre_ref, shift)


def first_step_kernel(shift, cut_ref, lo_ref, hi_ref, key_ref, geo_ref, latent_ref, square_edge_ref, pair_ref, wg_ref,
                      st_ref, rg_ref, acc_ref, wst_ref, wo_ref, pre_ref):
    wst_ref[...] = pair_ref[0, 0].T
    wo_ref[...] = square_edge_ref[0].T
    own = latent_ref.shape[0]
    latent = latent_ref[...]
    st_ref[:, own:] = jnp.zeros((st_ref.shape[0], st_ref.shape[1] - own), BF16)
    st_ref[:, :own] = mm_nt(wst_ref[...], latent).astype(BF16)
    fill_receivers(rg_ref, latent, pair_ref[0, 1].T, wg_ref)
    acc_ref[...] = jnp.zeros_like(acc_ref)
    edge_tiles(0, cut_ref[0], lo_ref, hi_ref, key_ref, geo_ref, st_ref, rg_ref, wo_ref, acc_ref, pre_ref, shift)


def second_kernel(shift, own_pad, halo_count, encoder, last, cut_ref, lo_ref, hi_ref, key_ref, geo_ref, *refs):
    halo_refs, refs = refs[:halo_count], refs[halo_count:]
    if encoder:
        embed_ref, square_grid_ref, *refs = refs
    st_own_ref, rg_ref, acc_in_ref, wst_ref, wo_ref, latent_ref, pair_ref, square_node_ref, *refs = refs
    if last:
        out_ref, st_ref, acc_ref, pre_ref = refs
    else:
        ids_ref, out_ref, send_ref, st_ref, acc_ref, pre_ref = refs
    st_ref[:, :own_pad] = st_own_ref[:, :own_pad]
    at = own_pad
    for halo_ref in halo_refs:
        rows = halo_ref.shape[0]
        if encoder:
            embed_grid(halo_ref, embed_ref, square_grid_ref, wst_ref, st_ref, at)
        else:
            st_ref[:, at : at + rows] = mm_nt(wst_ref[...], halo_ref[...]).astype(BF16)
        at += rows
    st_ref[:, at:] = jnp.zeros((st_ref.shape[0], st_ref.shape[1] - at), BF16)
    acc_ref[...] = acc_in_ref[...]
    edge_tiles(cut_ref[0], key_ref.shape[1] // TILE, lo_ref, hi_ref, key_ref, geo_ref, st_ref, rg_ref, wo_ref, acc_ref, pre_ref, shift)
    latent = latent_ref[...]
    pre_act = mm(latent, pair_ref[0, 2]) + mm(acc_ref[...].astype(BF16), pair_ref[0, 3])
    new = (latent.astype(F32) + norm(mm(silu_bf16(pre_act), square_node_ref[0]), 1)).astype(BF16)
    out_ref[...] = new
    if not last:
        pick_kernel(ids_ref, out_ref, send_ref)


def whole(shape):
    return pl.BlockSpec(shape, lambda i: (0,) * len(shape))


def block_of(array, index):
    shape = (1,) + array.shape[1:]
    return pl.BlockSpec(shape, lambda i: (index,) + (0,) * (len(shape) - 1))


SMEM = pl.BlockSpec(memory_space=pltpu.SMEM)


def call(body, ins, outs, scratch=()):
    arrays = [a for a, _ in ins]
    specs = [whole(a.shape) if s is None else s for a, s in ins]
    return pl.pallas_call(
        body,
        grid=(1,),
        in_specs=specs,
        out_specs=[whole(o.shape) for o in outs],
        out_shape=outs,
        scratch_shapes=list(scratch),
        compiler_params=pltpu.CompilerParams(vmem_limit_bytes=48 * 1024 * 1024),
    )(*arrays)


def shaped(shape, dtype):
    return jax.ShapeDtypeStruct(shape, dtype)


def pair_route(parity, lon_step):
    n_lat, n_lon = lax.axis_size("lat"), lax.axis_size("lon")
    route = []
    for lat in range(n_lat):
        other = lat + 1 if lat % 2 == parity else lat - 1
        if 0 <= other < n_lat:
            route += [(lat * n_lon + (lon - lon_step) % n_lon, other * n_lon + lon) for lon in range(n_lon)]
    return route


def lon_route(parity):
    n_lat, n_lon = lax.axis_size("lat"), lax.axis_size("lon")
    route = []
    for lat in range(n_lat):
        for lon in range(n_lon):
            other = (lon + 1 if lon % 2 == parity else lon - 1) % n_lon
            route.append((lat * n_lon + lon, lat * n_lon + other))
    return route


def order_edges(position, receivers, geometry, own_pad, shift):
    edges = receivers.shape[0]
    key, *geo = lax.sort(((position << shift) | receivers, *geometry), num_keys=1)
    features = jnp.stack(geo, axis=0)
    high = lax.reduce_precision(features, 8, 7)
    low = features - high
    geo_rows = jnp.concatenate(
        [high, low, high, jnp.zeros((GEO_ROWS - 3 * len(geo), edges), F32)], axis=0
    ).astype(BF16)
    sender = key >> shift
    tiles = sender.reshape(-1, TILE)
    lo, hi = tiles[:, 0], tiles[:, -1]
    cut = jnp.sum((hi < own_pad).astype(jnp.int32)).reshape(1)
    return [(cut, SMEM), (lo, SMEM), (hi, SMEM), (key.reshape(1, edges), None), (geo_rows, None)]


def per_device(
    grid_feat,
    grid_send,
    g2m_sender,
    g2m_receiver,
    g2m_geom,
    mesh_geom,
    mesh_adjacent_lists,
    mesh_far,
    mesh_sender,
    mesh_receiver,
    mesh_edge_geom,
    embed_in,
    mesh_in,
    geo_in,
    pair_in,
    square_out,
):
    width = embed_in.shape[1]
    own_grid = grid_feat.shape[0]
    slot = grid_send.shape[2]
    nodes = mesh_geom.shape[1]
    near = mesh_adjacent_lists.shape[2]
    far = mesh_far.shape[1] * mesh_far.shape[2]
    edges = mesh_sender.shape[0]
    shift = nodes.bit_length()
    lat_odd = lax.axis_index("lat") % 2
    lon_odd = lax.axis_index("lon") % 2

    high = lax.reduce_precision(geo_in, 8, 7)
    geo_columns = jnp.concatenate(
        [high, high, geo_in - high, jnp.zeros((geo_in.shape[0], GEO_ROWS - 3 * geo_in.shape[1], width), F32)], axis=1
    ).transpose(0, 2, 1).astype(BF16)

    lists = grid_send[0]
    order = [
        jnp.where(lat_odd == 1, lists[1], lists[0]),
        jnp.where(lat_odd == 1, lists[0], lists[1]),
        jnp.where(lon_odd == 1, lists[3], lists[2]),
        jnp.where(lon_odd == 1, lists[2], lists[3]),
    ]
    ids = jnp.stack(order).reshape(-1, LANES)
    (outgoing,) = call(
        pick_kernel, [(ids, None), (grid_feat, None)], [shaped((4 * slot, grid_feat.shape[1]), BF16)]
    )
    routes = [pair_route(1, 0), pair_route(0, 0), lon_route(1), lon_route(0)]
    arrived = [lax.ppermute(outgoing[i * slot : (i + 1) * slot], AXES, r) for i, r in enumerate(routes)]

    grid_pad = up(own_grid, LANES)
    offset = g2m_sender - own_grid
    side = offset // slot
    lat_slot = jnp.where((side == 0) == (lat_odd == 0), 1, 0)
    lon_slot = jnp.where((side == 2) == (lon_odd == 0), 3, 2)
    grid_slot = jnp.where(side < 2, lat_slot, lon_slot)
    position = jnp.where(g2m_sender < own_grid, g2m_sender, grid_pad + grid_slot * slot + offset % slot)
    encoder_edges = order_edges(position, g2m_receiver, g2m_geom, grid_pad, shift)

    rg_width = nodes + GEO_ROWS
    square = lambda k: (square_out, block_of(square_out, k))
    pre_scratch = pltpu.VMEM((width, TILE), F32)
    acc_shape = shaped((nodes, width), F32)
    weight_shape = shaped((width, width), BF16)

    st, rg, acc, wst, wo, latent = call(
        functools.partial(first_encoder_kernel, shift),
        encoder_edges
        + [(grid_feat, None), (mesh_geom.T, None), (embed_in, None), (mesh_in, None), square(0), square(1), square(2),
           (pair_in, block_of(pair_in, 0)), (geo_columns, block_of(geo_columns, 0))],
        [shaped((width, grid_pad + LANES), BF16), shaped((width, rg_width), BF16), acc_shape, weight_shape, weight_shape,
         shaped((nodes, width), BF16)],
        [pre_scratch],
    )

    near_lists = mesh_adjacent_lists[0]
    ahead, behind, beside = near_lists[5:8], near_lists[0:3], near_lists[3:5]
    near_order = jnp.concatenate([
        jnp.where(lat_odd == 1, ahead, behind),
        jnp.where(lat_odd == 1, behind, ahead),
        jnp.where(lon_odd == 1, beside[1:2], beside[0:1]),
        jnp.where(lon_odd == 1, beside[0:1], beside[1:2]),
    ]).reshape(-1)
    send_ids = jnp.concatenate([near_order, mesh_far[0].reshape(-1)])
    send_pad = up(send_ids.shape[0], LANES)
    send_ids = jnp.pad(send_ids, (0, send_pad - send_ids.shape[0])).reshape(-1, LANES)
    mesh_routes = [pair_route(1, v) for v in (-1, 0, 1)] + [pair_route(0, v) for v in (-1, 0, 1)]
    mesh_routes += [lon_route(1), lon_route(0)]

    mesh_pad = up(nodes, LANES)
    offset = mesh_sender - nodes
    side = offset // near
    up_side = side >= 5
    lat_slot = jnp.where(up_side == (lat_odd == 1), 3, 0) + jnp.where(up_side, side - 5, side)
    lon_slot = jnp.where((side == 3) == (lon_odd == 0), 7, 6)
    near_slot = jnp.where((side == 3) | (side == 4), lon_slot, lat_slot)
    halo_row = jnp.where(offset < 8 * near, near_slot * near + offset % near, offset)
    position = jnp.where(mesh_sender < nodes, mesh_sender, mesh_pad + halo_row)
    mesh_edges = order_edges(position, mesh_receiver, mesh_edge_geom, mesh_pad, shift)

    sections = geo_in.shape[0]
    halos = arrived
    for section in range(sections):
        encoder, last = section == 0, section == sections - 1
        if section > 0:
            st, rg, acc, wst, wo = call(
                functools.partial(first_step_kernel, shift),
                mesh_edges
                + [(latent, None), square(2 + 2 * section), (pair_in, block_of(pair_in, section)),
                   (geo_columns, block_of(geo_columns, section))],
                [shaped((width, mesh_pad + LANES), BF16), shaped((width, rg_width), BF16), acc_shape, weight_shape, weight_shape],
                [pre_scratch],
            )
        own_pad = grid_pad if encoder else mesh_pad
        halo_rows = sum(h.shape[0] for h in halos)
        ins = (encoder_edges if encoder else mesh_edges) + [(h, None) for h in halos]
        if encoder:
            ins += [(embed_in, None), square(0)]
        ins += [(st, None), (rg, None), (acc, None), (wst, None), (wo, None), (latent, None),
                (pair_in, block_of(pair_in, section)), square(3 + 2 * section)]
        outs = [shaped((nodes, width), BF16)]
        if not last:
            ins += [(send_ids, None)]
            outs += [shaped((send_pad, width), BF16)]
        scratch = [pltpu.VMEM((width, own_pad + up(halo_rows, LANES) + LANES), BF16), pltpu.VMEM((nodes, width), F32), pre_scratch]
        out = call(
            functools.partial(second_kernel, shift, own_pad, len(halos), encoder, last), ins, outs, scratch
        )
        latent = out[0]
        if not last:
            send = out[1]
            far_out = send[8 * near : 8 * near + far].reshape(mesh_far.shape[1], -1, width)
            far_in = lax.all_to_all(far_out, AXES, split_axis=0, concat_axis=0, tiled=True)
            halos = [lax.ppermute(send[i * near : (i + 1) * near], AXES, r) for i, r in enumerate(mesh_routes)]
            halos = [jnp.concatenate(halos, axis=0), far_in.reshape(-1, width)]
    return latent


def solution(mesh):
    in_specs = (
        P(("lat", "lon"), None),
        P(("lat", "lon"), None, None),
        P(("lat", "lon")),
        P(("lat", "lon")),
        P(None, ("lat", "lon")),
        P(None, ("lat", "lon")),
        P(("lat", "lon"), None, None),
        P(("lat", "lon"), None, None),
        P(("lat", "lon")),
        P(("lat", "lon")),
        P(None, ("lat", "lon")),
        P(),
        P(),
        P(),
        P(),
        P(),
    )
    out_specs = P(("lat", "lon"), None)
    return jax.shard_map(
        per_device, mesh=mesh, in_specs=in_specs, out_specs=out_specs, check_vma=False
    )
```

time: 310 us -> 193 us (0.62); the launches traced: 304 us -> 191 us
  local copies, waits for them, and re-layouts: 151 us -> 26.6 us
  Pallas kernels: 0 us -> 99.6 us
  matrix products: 96.8 us -> 0 us
  starting transfers between devices: 35.6 us -> 48 us
  waiting for transfers between devices: 11.2 us -> 1.21 us
  other arithmetic: 9.27 us -> 15.2 us
    gather x13 -> x0, local copies, waits for them, and re-layouts: 118 us -> none  [the longest x6 104 us: edge_sums(): pre_act = pre_act + sender_term[senders] + receiver_term[row_ids]]
    pallas_call x0 -> x7, Pallas kernels: none -> 99.6 us  [call(): pl.pallas_call(body, grid=(1,), in_specs=specs, out_specs=[whole(o.shape)...]
    dot_general x24 -> x0, matrix products: 96.8 us -> none  [the longest x3 33.7 us: edge_sums(): pre_act = jnp.dot(geometry.T, geo_weight, precision=lax.Precision.HIGHEST)]
    ppermute x12 -> x20, starting transfers between devices: 24 us -> 39.1 us  [the longest x16 31.1 us: per_device(): lax.ppermute(send[i * near:(i + 1) * near], AXES, r)]
    sort x0 -> x2, other arithmetic: none -> 12.5 us  [order_edges(): key, *geo = lax.sort((position << shift | receivers, *geometry), num_keys=1)]
    ppermute x12 -> x20, waiting for transfers between devices: 11.2 us -> 1.2 us  [the longest x16 1.19 us: per_device(): lax.ppermute(send[i * near:(i + 1) * near], AXES, r)]
    unnamed x68 -> x79, local copies, waits for them, and re-layouts: 26.8 us -> 21.3 us
    unnamed x4 -> x0, other arithmetic: 3.74 us -> none
  transfers between devices with their start and end apart: 14 -> 22, of which waited for: 4 -> 2; matrix products, arithmetic and copies ran while one was open for 28% -> 14% of each run, Pallas kernels for 0% -> 29%
where the time goes in v1:
time: 193 us; the launch traced here: 191 us
  Pallas kernels  99.6 us (52%)
  starting transfers between devices  48 us (25%)
  local copies, waits for them, and re-layouts  26.6 us (14%)
  other arithmetic  15.2 us (8%)
    pallas_call x7, Pallas kernels, call(): pl.pallas_call(body, grid=(1,), in_specs=specs, out_specs=[whole(o.shape)...  99.6 us
    ppermute x16, starting transfers between devices, per_device(): lax.ppermute(send[i * near:(i + 1) * near], AXES, r)  31.1 us
    unnamed x79, local copies, waits for them, and re-layouts  21.3 us
    sort x2, other arithmetic, order_edges(): key, *geo = lax.sort((position << shift | receivers, *geometry), num_keys=1)  12.5 us
    all_to_all x2, starting transfers between devices, per_device(): lax.all_to_all(far_out, AXES, split_axis=0, concat_axis=0, tiled=True)  8.81 us
    ppermute x4, starting transfers between devices, per_device(): lax.ppermute(outgoing[i * slot:(i + 1) * slot], AXES, r)  8.08 us
  transfers between devices with their start and end apart: 22, of which 2 were waited for; matrix products, arithmetic and copies ran while one was open for 14% of the time, Pallas kernels for 29%

profile of v1, /device:TPU:0, one launch (start us, length us, event | category | flops | bytes accessed | tf_op | source)
XLA Modules:
  0.0 191.1 jit_solution(13593801449153548650)
XLA Ops:
  0.1 1.6 copy.35.table_ref.grid_ref
  2.6 1.4 shard_map.154
  5.7 5.8 %collective-permute-start.1 = (bf16[256,474]{1,0:T(8,128)(2,1)}, bf16[256,474]{1,0:T(8,128)(2,1)S(1)}, u32[]{:S(2)}, u32[]{:S(2)}) collective-permute-start(bf16[256,474]{1,0:T(8,128)(2,1)} %get-tuple-element.97), channel_id=1, source_target_pairs={{0,4},{1,5},{2,6},{3,7},{4,0},{5,1},{6,2},{7,3},{8,12},{9,13},{10,... | collective-permute-start | bytes 728072 | tf_op jit(solution)/shard_map/ppermute | solution.py:282
  13.4 6.2 %sort.95 = (s32[4096]{0:T(1024)S(1)}, f32[4096]{0:T(1024)S(1)}, f32[4096]{0:T(1024)S(1)}, f32[4096]{0:T(1024)S(1)}, f32[4096]{0:T(1024)S(1)}, /*index=5*/s32[4096]{0:T(1024)}) sort(s32[4096]{0:T(1024)S(1)} %get-tuple-element.124, f32[4096]{0:T(1024)S(1)} %bitcast.56, f32[4096]{0:T(1024)S(1)} %bitcast.55, f32[4096]{0:T(1024)S(1)} %bitcast.57, ...), dimensions={0}, to_apply=%region_2.3 | sort | flops 49152 | bytes 196608 | tf_op jit(solution)/shard_map/sort | solution.py:222
  19.8 6.2 %sort.94 = (s32[4096]{0:T(1024)S(1)}, f32[4096]{0:T(1024)S(1)}, f32[4096]{0:T(1024)S(1)}, f32[4096]{0:T(1024)S(1)}, f32[4096]{0:T(1024)S(1)}, /*index=5*/s32[4096]{0:T(1024)}) sort(s32[4096]{0:T(1024)S(1)} %get-tuple-element.123, f32[4096]{0:T(1024)S(1)} %bitcast.52, f32[4096]{0:T(1024)S(1)} %bitcast.51, f32[4096]{0:T(1024)S(1)} %bitcast.53, ...), dimensions={0}, to_apply=%region_0.1 | sort | flops 49152 | bytes 196608 | tf_op jit(solution)/shard_map/sort | solution.py:222
  27.9 19.9 %shard_map.155 = (bf16[512,1152]{1,0:T(8,128)(2,1)S(1)}, bf16[512,336]{1,0:T(8,128)(2,1)S(1)}, f32[320,512]{1,0:T(8,128)S(1)}, bf16[512,512]{1,0:T(8,128)(2,1)S(...) custom-call(s32[1]{0:T(128)} %bitcast.14.cut_ref, s32[16]{0:T(128)S(1)} %get-tuple-element.75.lo_ref, ...), custom_call_target="tpu_custom_call" | custom-call | tf_op jit(solution)/shard_map/pallas_call | solution.py:185
  48.9 17.4 %shard_map.156 = (bf16[320,512]{1,0:T(8,128)(2,1)S(1)}, bf16[1024,512]{1,0:T(8,128)(2,1)S(1)}) custom-call(s32[1]{0:T(128)} %bitcast.14.cut_ref, s32[16]{0:T(128)S(1)} %get-tuple-element.75.lo_ref, s32[16]{0:T(128)S(1)} %get-tuple-element.76.hi_ref, s32[1,4096]{1,0:T(1,128)S(1)} %bitcast.49, bf16[16,4096]{1,0:T(8,128)(2,1)S(1)} %get-tuple-element.121.geo_ref, ...), custom_call_target="tpu_custom_call" | custom-call | tf_op jit(solution)/shard_map/pallas_call | solution.py:185
  67.2 1.3 collective-permute-start.4
  69.4 1.3 collective-permute-start.5
  70.7 1.3 collective-permute-start.6
  72.0 7.8 %collective-permute-start.7 = (bf16[112,512]{1,0:T(8,128)(2,1)}, bf16[112,512]{1,0:T(8,128)(2,1)}, u32[]{:S(2)}, u32[]{:S(2)}) collective-permute-start(bf16[112,512]{1,0:T(8,128)(2,1)} %get-tuple-element.91), channel_id=1, source_target_pairs={{1,4},{2,5},{3,6},{0,7},{5,0},{6,1},{7,2},{4,3},{9,12},{10,13},{11... | collective-permute-start | bytes 344072 | tf_op jit(solution)/shard_map/ppermute | solution.py:367
  80.5 5.1 %all-to-all-start = ((bf16[32,4,512]{2,1,0:T(4,128)(2,1)}), bf16[32,4,512]{2,1,0:T(4,128)(2,1)S(1)}, u32[]{:S(2)}, u32[]{:S(2)}) async-start(bf16[32,4,512]{2,1,0:T(4,128)(2,1)} %reshape.185), calls=%async_computation | async-start | bytes 262144 | tf_op jit(solution)/shard_map/all_to_all | solution.py:366
  85.6 17.7 %shard_map.157 = (bf16[512,512]{1,0:T(8,128)(2,1)S(1)}, bf16[512,336]{1,0:T(8,128)(2,1)S(1)}, f32[320,512]{1,0:T(8,128)S(1)}, bf16[512,512]{1,0:T(8,128)(2,1)S(1)}, bf16[512,512]{1,0:T(8,128)(2,1)S(1)}) custom-call(s32[1]{0:T(128)} %bitcast.4.cut_ref, s32[16]{0:T(128)S(1)} %get-tuple-element.77.lo_ref, s32[16]{0:T(128)S(1)} %get-tuple-element.78.hi_ref, ...), custom_call_target="tpu_custom_call" | custom-call | tf_op jit(solution)/shard_map/pallas_call | solution.py:185
  104.6 1.5 collective-permute-start.10
  113.8 13.2 %shard_map.158 = (bf16[320,512]{1,0:T(8,128)(2,1)S(1)}, bf16[1024,512]{1,0:T(8,128)(2,1)S(1)}) custom-call(s32[1]{0:T(128)} %bitcast.4.cut_ref, s32[16]{0:T(128)S(1)} %get-tuple-element.77.lo_ref, s32[16]{0:T(128)S(1)} %get-tuple-element.78.hi_ref, s32[1,4096]{1,0:T(1,128)S(1)} %bitcast.45, bf16[16,4096]{1,0:T(8,128)(2,1)S(1)} %get-tuple-element.122.geo_ref, ...), custom_call_target="tpu_custom_call" | custom-call | tf_op jit(solution)/shard_map/pallas_call | solution.py:185
  127.9 1.3 collective-permute-start.12
  129.2 1.3 collective-permute-start.13
  130.5 1.3 collective-permute-start.14
  131.8 10.1 %collective-permute-start.15 = (bf16[112,512]{1,0:T(8,128)(2,1)}, bf16[112,512]{1,0:T(8,128)(2,1)}, u32[]{:S(2)}, u32[]{:S(2)}) collective-permute-start(bf16[112,512]{1,0:T(8,128)(2,1)} %get-tuple-element.83), channel_id=1, source_target_pairs={{1,4},{2,5},{3,6},{0,7},{5,0},{6,1},{7,2},{4,3},{9,12},{10,13},{11... | collective-permute-start | bytes 344072 | tf_op jit(solution)/shard_map/ppermute | solution.py:367
  141.9 17.6 %shard_map.159 = (bf16[512,512]{1,0:T(8,128)(2,1)S(1)}, bf16[512,336]{1,0:T(8,128)(2,1)S(1)}, f32[320,512]{1,0:T(8,128)S(1)}, bf16[512,512]{1,0:T(8,128)(2,1)S(1)}, bf16[512,512]{1,0:T(8,128)(2,1)S(1)}) custom-call(s32[1]{0:T(128)} %bitcast.4.cut_ref, s32[16]{0:T(128)S(1)} %get-tuple-element.77.lo_ref, s32[16]{0:T(128)S(1)} %get-tuple-element.78.hi_ref, ...), custom_call_target="tpu_custom_call" | custom-call | tf_op jit(solution)/shard_map/pallas_call | solution.py:185
  161.9 3.8 %all-to-all-start.1 = ((bf16[32,4,512]{2,1,0:T(4,128)(2,1)}), bf16[32,4,512]{2,1,0:T(4,128)(2,1)S(1)}, u32[]{:S(2)}, u32[]{:S(2)}) async-start(bf16[32,4,512]{2,1,0:T(4,128)(2,1)} %reshape.187), calls=%async_computation.1 | async-start | bytes 262144 | tf_op jit(solution)/shard_map/all_to_all | solution.py:366
  165.7 1.6 collective-permute-start.17
  168.2 1.5 collective-permute-start.18
  178.7 12.5 %shard_map.160 = bf16[320,512]{1,0:T(8,128)(2,1)} custom-call(s32[1]{0:T(128)} %bitcast.4.cut_ref, s32[16]{0:T(128)S(1)} %copy-done.15, s32[16]{0:T(128)S(1)} %copy-done.17, s32[1,4096]{1,0:T(1,128)S(1)} %bitcast.47, bf16[16,4096]{1,0:T(8,128)(2,1)S(1)} %get-tuple-element.122.geo_ref, bf16[896,512]{1,0:T(8,128)(2,1)S(1)} %constant_dynamic-update-slice_fusion.8.refs_0_, ...), custom_call_target="tpu_custom_call" | custom-call | tf_op jit(solution)/shard_map/pallas_call | solution.py:185
  (149 shorter events, 32.0 us)
Async XLA Ops:
  5.0 43.9 %collective-permute-start = (bf16[256,474]{1,0:T(8,128)(2,1)}, bf16[256,474]{1,0:T(8,128)(2,1)S(1)}, u32[]{:S(2)}, u32[]{:S(2)}) collective-permute-start(bf16[256,474]{1,0:T(8,128)(2,1)} %get-tuple-element.98), channel_id=1, source_target_pairs={{4,8},{5,9},{6,10},{7,11},{8,4},{9,5},{10,6},{11,7},{12,16},{13,17... | collective-permute-start | bytes 728072 | tf_op jit(solution)/shard_map/ppermute | solution.py:282
  5.7 43.2 %collective-permute-start.1 = (bf16[256,474]{1,0:T(8,128)(2,1)}, bf16[256,474]{1,0:T(8,128)(2,1)S(1)}, u32[]{:S(2)}, u32[]{:S(2)}) collective-permute-start(bf16[256,474]{1,0:T(8,128)(2,1)} %get-tuple-element.97), channel_id=1, source_target_pairs={{0,4},{1,5},{2,6},{3,7},{4,0},{5,1},{6,2},{7,3},{8,12},{9,13},{10,... | collective-permute-start | bytes 728072 | tf_op jit(solution)/shard_map/ppermute | solution.py:282
  11.4 37.5 %collective-permute-start.2 = (bf16[256,474]{1,0:T(8,128)(2,1)}, bf16[256,474]{1,0:T(8,128)(2,1)S(1)}, u32[]{:S(2)}, u32[]{:S(2)}) collective-permute-start(bf16[256,474]{1,0:T(8,128)(2,1)} %get-tuple-element.96), channel_id=1, source_target_pairs={{0,3},{1,2},{2,1},{3,0},{4,7},{5,6},{6,5},{7,4},{8,11},{9,10},{10,... | collective-permute-start | bytes 728072 | tf_op jit(solution)/shard_map/ppermute | solution.py:282
  11.8 37.1 %collective-permute-start.3 = (bf16[256,474]{1,0:T(8,128)(2,1)}, bf16[256,474]{1,0:T(8,128)(2,1)S(1)}, u32[]{:S(2)}, u32[]{:S(2)}) collective-permute-start(bf16[256,474]{1,0:T(8,128)(2,1)} %get-tuple-element.95), channel_id=1, source_target_pairs={{0,1},{1,0},{2,3},{3,2},{4,5},{5,4},{6,7},{7,6},{8,9},{9,8},{10,11... | collective-permute-start | bytes 728072 | tf_op jit(solution)/shard_map/ppermute | solution.py:282
  67.2 36.0 %collective-permute-start.4 = (bf16[112,512]{1,0:T(8,128)(2,1)S(1)}, bf16[112,512]{1,0:T(8,128)(2,1)}, u32[]{:S(2)}, u32[]{:S(2)}) collective-permute-start(bf16[112,512]{1,0:T(8,128)(2,1)S(1)} %get-tuple-element.94), channel_id=1, source_target_pairs={{5,8},{6,9},{7,10},{4,11},{9,4},{10,5},{11,6},{8,7},{13,16},{14,17... | collective-permute-start | bytes 344072 | tf_op jit(solution)/shard_map/ppermute | solution.py:367
  68.7 73.2 %copy-start.14 = (s32[16]{0:T(128)}, s32[16]{0:T(128)S(1)}, u32[]{:S(2)}) copy-start(s32[16]{0:T(128)S(1)} %get-tuple-element.77.lo_ref) | copy-start | bytes 196
  68.7 73.2 %copy-start.16 = (s32[16]{0:T(128)}, s32[16]{0:T(128)S(1)}, u32[]{:S(2)}) copy-start(s32[16]{0:T(128)S(1)} %get-tuple-element.78.hi_ref) | copy-start | bytes 196
  69.4 35.2 %collective-permute-start.5 = (bf16[112,512]{1,0:T(8,128)(2,1)}, bf16[112,512]{1,0:T(8,128)(2,1)}, u32[]{:S(2)}, u32[]{:S(2)}) collective-permute-start(bf16[112,512]{1,0:T(8,128)(2,1)} %get-tuple-element.93), channel_id=1, source_target_pairs={{4,8},{5,9},{6,10},{7,11},{8,4},{9,5},{10,6},{11,7},{12,16},{13,17... | collective-permute-start | bytes 344072 | tf_op jit(solution)/shard_map/ppermute | solution.py:367
  70.7 36.2 %collective-permute-start.6 = (bf16[112,512]{1,0:T(8,128)(2,1)}, bf16[112,512]{1,0:T(8,128)(2,1)}, u32[]{:S(2)}, u32[]{:S(2)}) collective-permute-start(bf16[112,512]{1,0:T(8,128)(2,1)} %get-tuple-element.92), channel_id=1, source_target_pairs={{7,8},{4,9},{5,10},{6,11},{11,4},{8,5},{9,6},{10,7},{15,16},{12,17... | collective-permute-start | bytes 344072 | tf_op jit(solution)/shard_map/ppermute | solution.py:367
  72.0 36.2 %collective-permute-start.7 = (bf16[112,512]{1,0:T(8,128)(2,1)}, bf16[112,512]{1,0:T(8,128)(2,1)}, u32[]{:S(2)}, u32[]{:S(2)}) collective-permute-start(bf16[112,512]{1,0:T(8,128)(2,1)} %get-tuple-element.91), channel_id=1, source_target_pairs={{1,4},{2,5},{3,6},{0,7},{5,0},{6,1},{7,2},{4,3},{9,12},{10,13},{11... | collective-permute-start | bytes 344072 | tf_op jit(solution)/shard_map/ppermute | solution.py:367
  79.8 29.3 %collective-permute-start.8 = (bf16[112,512]{1,0:T(8,128)(2,1)}, bf16[112,512]{1,0:T(8,128)(2,1)}, u32[]{:S(2)}, u32[]{:S(2)}) collective-permute-start(bf16[112,512]{1,0:T(8,128)(2,1)} %get-tuple-element.90), channel_id=1, source_target_pairs={{0,4},{1,5},{2,6},{3,7},{4,0},{5,1},{6,2},{7,3},{8,12},{9,13},{10,... | collective-permute-start | bytes 344072 | tf_op jit(solution)/shard_map/ppermute | solution.py:367
  80.5 30.2 %all-to-all-start = ((bf16[32,4,512]{2,1,0:T(4,128)(2,1)}), bf16[32,4,512]{2,1,0:T(4,128)(2,1)S(1)}, u32[]{:S(2)}, u32[]{:S(2)}) async-start(bf16[32,4,512]{2,1,0:T(4,128)(2,1)} %reshape.185), calls=%async_computation | async-start | bytes 262144 | tf_op jit(solution)/shard_map/all_to_all | solution.py:366
  103.3 6.8 %collective-permute-start.9 = (bf16[112,512]{1,0:T(8,128)(2,1)}, bf16[112,512]{1,0:T(8,128)(2,1)S(1)}, u32[]{:S(2)}, u32[]{:S(2)}) collective-permute-start(bf16[112,512]{1,0:T(8,128)(2,1)} %get-tuple-element.89), channel_id=1, source_target_pairs={{3,4},{0,5},{1,6},{2,7},{7,0},{4,1},{5,2},{6,3},{11,12},{8,13},{9,... | collective-permute-start | bytes 344072 | tf_op jit(solution)/shard_map/ppermute | solution.py:367
  104.6 6.0 %collective-permute-start.10 = (bf16[112,512]{1,0:T(8,128)(2,1)S(1)}, bf16[112,512]{1,0:T(8,128)(2,1)S(1)}, u32[]{:S(2)}, u32[]{:S(2)}) collective-permute-start(bf16[112,512]{1,0:T(8,128)(2,1)S(1)} %copy-done.20), channel_id=1, source_target_pairs={{0,3},{1,2},{2,1},{3,0},{4,7},{5,6},{6,5},{7,4},{8,11},{9,10},{10,... | collective-permute-start | bytes 344072 | tf_op jit(solution)/shard_map/ppermute | solution.py:367
  107.0 3.6 %collective-permute-start.11 = (bf16[112,512]{1,0:T(8,128)(2,1)S(1)}, bf16[112,512]{1,0:T(8,128)(2,1)S(1)}, u32[]{:S(2)}, u32[]{:S(2)}) collective-permute-start(bf16[112,512]{1,0:T(8,128)(2,1)S(1)} %copy-done.19), channel_id=1, source_target_pairs={{0,1},{1,0},{2,3},{3,2},{4,5},{5,4},{6,7},{7,6},{8,9},{9,8},{10,11... | collective-permute-start | bytes 344072 | tf_op jit(solution)/shard_map/ppermute | solution.py:367
  127.9 37.8 %collective-permute-start.12 = (bf16[112,512]{1,0:T(8,128)(2,1)S(1)}, bf16[112,512]{1,0:T(8,128)(2,1)}, u32[]{:S(2)}, u32[]{:S(2)}) collective-permute-start(bf16[112,512]{1,0:T(8,128)(2,1)S(1)} %get-tuple-element.86), channel_id=1, source_target_pairs={{5,8},{6,9},{7,10},{4,11},{9,4},{10,5},{11,6},{8,7},{13,16},{14,17... | collective-permute-start | bytes 344072 | tf_op jit(solution)/shard_map/ppermute | solution.py:367
  129.2 39.0 %collective-permute-start.13 = (bf16[112,512]{1,0:T(8,128)(2,1)}, bf16[112,512]{1,0:T(8,128)(2,1)}, u32[]{:S(2)}, u32[]{:S(2)}) collective-permute-start(bf16[112,512]{1,0:T(8,128)(2,1)} %get-tuple-element.85), channel_id=1, source_target_pairs={{4,8},{5,9},{6,10},{7,11},{8,4},{9,5},{10,6},{11,7},{12,16},{13,17... | collective-permute-start | bytes 344072 | tf_op jit(solution)/shard_map/ppermute | solution.py:367
  130.5 40.1 %collective-permute-start.14 = (bf16[112,512]{1,0:T(8,128)(2,1)}, bf16[112,512]{1,0:T(8,128)(2,1)}, u32[]{:S(2)}, u32[]{:S(2)}) collective-permute-start(bf16[112,512]{1,0:T(8,128)(2,1)} %get-tuple-element.84), channel_id=1, source_target_pairs={{7,8},{4,9},{5,10},{6,11},{11,4},{8,5},{9,6},{10,7},{15,16},{12,17... | collective-permute-start | bytes 344072 | tf_op jit(solution)/shard_map/ppermute | solution.py:367
  131.8 39.9 %collective-permute-start.15 = (bf16[112,512]{1,0:T(8,128)(2,1)}, bf16[112,512]{1,0:T(8,128)(2,1)}, u32[]{:S(2)}, u32[]{:S(2)}) collective-permute-start(bf16[112,512]{1,0:T(8,128)(2,1)} %get-tuple-element.83), channel_id=1, source_target_pairs={{1,4},{2,5},{3,6},{0,7},{5,0},{6,1},{7,2},{4,3},{9,12},{10,13},{11... | collective-permute-start | bytes 344072 | tf_op jit(solution)/shard_map/ppermute | solution.py:367
  141.9 30.7 %collective-permute-start.16 = (bf16[112,512]{1,0:T(8,128)(2,1)}, bf16[112,512]{1,0:T(8,128)(2,1)}, u32[]{:S(2)}, u32[]{:S(2)}) collective-permute-start(bf16[112,512]{1,0:T(8,128)(2,1)} %get-tuple-element.82), channel_id=1, source_target_pairs={{0,4},{1,5},{2,6},{3,7},{4,0},{5,1},{6,2},{7,3},{8,12},{9,13},{10,... | collective-permute-start | bytes 344072 | tf_op jit(solution)/shard_map/ppermute | solution.py:367
  161.9 12.4 %all-to-all-start.1 = ((bf16[32,4,512]{2,1,0:T(4,128)(2,1)}), bf16[32,4,512]{2,1,0:T(4,128)(2,1)S(1)}, u32[]{:S(2)}, u32[]{:S(2)}) async-start(bf16[32,4,512]{2,1,0:T(4,128)(2,1)} %reshape.187), calls=%async_computation.1 | async-start | bytes 262144 | tf_op jit(solution)/shard_map/all_to_all | solution.py:366
  165.7 7.9 %collective-permute-start.17 = (bf16[112,512]{1,0:T(8,128)(2,1)}, bf16[112,512]{1,0:T(8,128)(2,1)S(1)}, u32[]{:S(2)}, u32[]{:S(2)}) collective-permute-start(bf16[112,512]{1,0:T(8,128)(2,1)} %get-tuple-element.81), channel_id=1, source_target_pairs={{3,4},{0,5},{1,6},{2,7},{7,0},{4,1},{5,2},{6,3},{11,12},{8,13},{9,... | collective-permute-start | bytes 344072 | tf_op jit(solution)/shard_map/ppermute | solution.py:367
  168.2 6.0 %collective-permute-start.18 = (bf16[112,512]{1,0:T(8,128)(2,1)S(1)}, bf16[112,512]{1,0:T(8,128)(2,1)S(1)}, u32[]{:S(2)}, u32[]{:S(2)}) collective-permute-start(bf16[112,512]{1,0:T(8,128)(2,1)S(1)} %get-tuple-element.80), channel_id=1, source_target_pairs={{0,3},{1,2},{2,1},{3,0},{4,7},{5,6},{6,5},{7,4},{8,11},{9,10},{10,... | collective-permute-start | bytes 344072 | tf_op jit(solution)/shard_map/ppermute | solution.py:367
  170.6 3.6 %collective-permute-start.19 = (bf16[112,512]{1,0:T(8,128)(2,1)S(1)}, bf16[112,512]{1,0:T(8,128)(2,1)S(1)}, u32[]{:S(2)}, u32[]{:S(2)}) collective-permute-start(bf16[112,512]{1,0:T(8,128)(2,1)S(1)} %get-tuple-element.79), channel_id=1, source_target_pairs={{0,1},{1,0},{2,3},{3,2},{4,5},{5,4},{6,7},{7,6},{8,9},{9,8},{10,11... | collective-permute-start | bytes 344072 | tf_op jit(solution)/shard_map/ppermute | solution.py:367
  (29 other events, 298.7 us)
